TPU v7x, 32 devices: a whole 2x2x4 slice. The times are simulated.
32 devices in a mesh: ka: 4 (over y, x), pw: 8 (over z, core).
Axes of the slice: x: 2, y: 2, z: 4, core: 2. Of those that a mesh axis runs over, the one named last changes fastest.
Arguments:
- states_re: bfloat16 [8, 512, 32768], P('ka', None, 'pw'), may hold values from -0.016572815 to 0.016572815
- states_im: bfloat16 [8, 512, 32768], P('ka', None, 'pw'), may hold values from -0.016572815 to 0.016572815
Outputs:
- wilson_lines: float32 [8, 512, 2, 512], P('ka', 'pw')
All inputs are finite; a program needn't handle non-finite values.
Results may differ from a plain program's by a relative error of at most 0.0003.
Values may be sent and summed in bfloat16 or wider, within the bound.
No kernel may reach another device: no remote copies, remote signals or barrier semaphores. Data moves between devices by JAX's collectives and lax.ppermute only.
A program may use at most 128 MiB of HBM per device.

v0:
```python
import jax
import jax.numpy as jnp
from jax import lax
from jax.sharding import PartitionSpec as P


def exact_dot(left, right):
    return jnp.dot(left, right, precision=lax.Precision.HIGH, preferred_element_type=jnp.float32)


def packed(states_re, states_im, kpoint, first, width):
    parts = [s[kpoint, first : first + width] for s in (states_re, states_im)]
    return jnp.concatenate(parts, 0)


def margin_of(own, other):
    bands = own.shape[0] // 2
    width = other.shape[0] // 2
    dots = lax.dot_general(own, other, (((1,), (1,)), ((), ())), preferred_element_type=jnp.float32)
    real_part = dots[:bands, :width] + dots[bands:, width:]
    imag_part = dots[:bands, width:] - dots[bands:, :width]
    return real_part, imag_part


def block_form(matrix):
    bands = matrix.shape[0]
    real_part, imag_part = matrix[:, :bands], matrix[:, bands:]
    return jnp.concatenate(
        [jnp.concatenate([real_part, -imag_part], 1), jnp.concatenate([imag_part, real_part], 1)], 0
    )


def rows_times(rows, matrix):
    _, count, bands = rows.shape
    dots = exact_dot(rows.reshape(2 * count, bands), matrix)
    real_part = dots[:count, :bands] - dots[count:, bands:]
    imag_part = dots[:count, bands:] + dots[count:, :bands]
    return jnp.stack([real_part, imag_part], 0)


def after(value, earlier):
    return lax.optimization_barrier((value, earlier))[0]


def shards(states_re, states_im):
    kcount, bands, _ = states_re.shape
    ka_width = lax.axis_size("ka")
    pw_width = lax.axis_size("pw")
    band_rows = bands // pw_width
    ka_place = lax.axis_index("ka")
    first_band = lax.axis_index("pw") * band_rows
    eighth = bands // 8
    widths = [eighth, 2 * eighth, 2 * eighth, 2 * eighth, eighth]
    firsts = [sum(widths[:i]) for i in range(len(widths))]

    to_previous = [(i, (i - 1) % ka_width) for i in range(ka_width)]
    arrivals = []
    for number, (first, width) in enumerate(zip(firsts, widths)):
        block = packed(states_re, states_im, 0, first, width)
        if number >= 2:
            block = after(block, arrivals[number - 2])
        arrivals.append(lax.ppermute(block, "ka", to_previous))

    states_re, states_im = after((states_re, states_im), arrivals[0])
    whole = [packed(states_re, states_im, k, 0, bands) for k in range(kcount)]
    own_margins = []
    before = None
    for k in range(kcount - 1):
        margin = lax.psum(jnp.concatenate(margin_of(whole[k], whole[k + 1]), 1), "pw")
        if before is not None:
            before = rows_times(jnp.stack([before[:, :bands], before[:, bands:]]), margin)
            margin = jnp.concatenate([before[0], before[1]], 1)
        before = margin
        own_margins.append(margin)
    left = None if before is None else block_form(after(before, arrivals[1]))

    sections = []
    last_dots = None
    for block in arrivals:
        if last_dots is not None:
            block = after(block, last_dots)
        real_part, imag_part = margin_of(whole[kcount - 1], block)
        last_dots = real_part
        if left is not None:
            product = exact_dot(left, jnp.concatenate([real_part, imag_part], 0))
            real_part, imag_part = product[:bands], product[bands:]
        section = jnp.concatenate([real_part, imag_part], 1)
        if sections:
            section = after(section, sections[-1])
        sections.append(lax.psum(section, "pw"))
    reals = [section[:, : section.shape[1] // 2] for section in sections]
    imags = [section[:, section.shape[1] // 2 :] for section in sections]
    span = jnp.concatenate(reals + imags, 1)

    line = lax.dynamic_slice_in_dim(span, first_band, band_rows, 0)
    line = jnp.stack([line[:, :bands], line[:, bands:]], 0)
    row_index = lax.broadcasted_iota(jnp.int32, (band_rows, bands), 0) + first_band
    col_index = lax.broadcasted_iota(jnp.int32, (band_rows, bands), 1)
    eye_real = (row_index == col_index).astype(jnp.float32)
    start = jnp.stack([eye_real, jnp.zeros_like(eye_real)], 0)
    for place in range(1, ka_width):
        received = lax.ppermute(line, "ka", [(place - 1, place)])
        start = jnp.where(ka_place == place, received, start)
        if place < ka_width - 1:
            line = rows_times(start, span)

    lines = [rows_times(start, matrix) for matrix in own_margins + [span]]
    return jnp.stack([jnp.moveaxis(one, 0, 1) for one in lines], 0)


def solution(mesh):
    in_specs = (P("ka", None, "pw"), P("ka", None, "pw"))
    out_specs = P("ka", "pw", None, None)
    return jax.shard_map(shards, mesh=mesh, in_specs=in_specs, out_specs=out_specs, check_vma=False)
```

profile of v0, /device:TPU:6, one launch (start us, length us, event | category | flops | bytes accessed | tf_op | source)
XLA Modules:
  0.0 484.2 jit_solution(12773956809166216955)
XLA Ops:
  6.5 1.7 slice_bitcast_fusion.10
  8.9 3.4 slice_bitcast_fusion.4
  12.3 1.5 pad_maximum_fusion.2
  13.7 1.4 collective-permute-start.1
  15.4 1.5 pad_maximum_fusion.4
  16.9 18.4 %collective-permute-done = bf16[128,4096]{1,0:T(8,128)(2,1)S(1)} collective-permute-done((bf16[128,4096]{1,0:T(8,128)(2,1)S(1)}, bf16[128,4096]{1,0:T(8,128)(2,1)S(1)}, u32[]{:S(2)}, u32[]{:S(2)}) %collective-permute-start) | collective-permute-done | bytes 1048608 | tf_op jit(solution)/shard_map/ppermute | solution.py:62
  35.3 3.6 slice_bitcast_fusion.2
  38.9 3.6 slice_bitcast_fusion.3
  42.4 16.6 %fusion = f32[1024,1024]{0,1:T(8,128)} fusion(bf16[512,4096]{1,0:T(8,128)(2,1)} %get-tuple-element.45, bf16[512,4096]{1,0:T(8,128)(2,1)} %get-tuple-element.43, bf16[512,4096]{1,0:T(8,128)(2,1)} %get-tuple-element.46, bf16[512,4096]{1,0:T(8,128)(2,1)} %get-tuple-element.44), kind=kOutput, calls=%fused_computation | convolution fusion | flops 8623489024 | bytes 20971520 | tf_op jit(solution)/shard_map/dot_general | solution.py:19
  59.1 2.6 slice_add_fusion
  61.7 1.5 pad_maximum_fusion.1
  63.3 1.1 pad_maximum_fusion.6
  64.4 6.6 %fusion.42 = f32[1024,128]{0,1:T(8,128)S(1)} fusion(bf16[128,4096]{1,0:T(8,128)(2,1)} %copy-done.12, bf16[512,4096]{1,0:T(8,128)(2,1)} %get-tuple-element.46, bf16[512,4096]{1,0:T(8,128)(2,1)} %get-tuple-element.44), kind=kOutput, calls=%fused_computation.113 | convolution fusion | flops 1090519040 | bytes 9961472 | tf_op jit(solution)/shard_map/dot_general | solution.py:19
  71.0 58.6 %all-reduce.8.cloned.1.call-done = f32[512,1024]{0,1:T(8,128)} async-done(((f32[512,1024]{0,1:T(8,128)}), f32[512,1024]{0,1:T(8,128)}) %all-reduce.8.cloned.1.call-update) | async-done | bytes 2097168 | tf_op jit(solution)/shard_map/psum | solution.py:69
  129.6 1.8 slice_negate_fusion
  131.5 1.0 copy-done.1
  132.4 1.3 fusion.20
  134.6 6.6 %fusion.41 = f32[1024,256]{1,0:T(8,128)S(1)} fusion(bf16[256,4096]{1,0:T(8,128)(2,1)} %collective-permute-done.1, bf16[512,4096]{1,0:T(8,128)(2,1)} %get-tuple-element.46, bf16[512,4096]{1,0:T(8,128)(2,1)} %get-tuple-element.44), kind=kOutput, calls=%fused_computation.112 | convolution fusion | flops 2164260864 | bytes 11534336 | tf_op jit(solution)/shard_map/dot_general | solution.py:19
  141.2 1.3 fusion.4
  144.0 45.1 %all-reduce.10.cloned.1.call-done = f32[512,128]{0,1:T(8,128)} async-done(((f32[512,128]{0,1:T(8,128)}), f32[512,128]{0,1:T(8,128)}) %all-reduce.10.cloned.1.call-update) | async-done | bytes 262160 | tf_op jit(solution)/shard_map/psum | solution.py:90
  189.2 6.6 %fusion.40 = f32[1024,256]{1,0:T(8,128)S(1)} fusion(bf16[256,4096]{1,0:T(8,128)(2,1)} %collective-permute-done.2, bf16[512,4096]{1,0:T(8,128)(2,1)} %get-tuple-element.46, bf16[512,4096]{1,0:T(8,128)(2,1)} %get-tuple-element.44), kind=kOutput, calls=%fused_computation.111 | convolution fusion | flops 2164260864 | bytes 11534336 | tf_op jit(solution)/shard_map/dot_general | solution.py:19
  195.9 1.3 fusion.8
  197.2 0.9 pad_maximum_fusion.8
  198.1 48.6 %all-reduce.12.cloned.1.call-done = f32[512,256]{0,1:T(8,128)} async-done(((f32[512,256]{0,1:T(8,128)}), f32[512,256]{0,1:T(8,128)}) %all-reduce.12.cloned.1.call-update) | async-done | bytes 524304 | tf_op jit(solution)/shard_map/psum | solution.py:90
  246.8 1.0 slice_dynamic-update-slice_fusion.5
  248.6 55.4 %all-reduce.14.cloned.1.call-done = f32[512,256]{0,1:T(8,128)} async-done(((f32[512,256]{0,1:T(8,128)}), f32[512,256]{0,1:T(8,128)}) %all-reduce.14.cloned.1.call-update) | async-done | bytes 524304 | tf_op jit(solution)/shard_map/psum | solution.py:90
  304.0 1.0 slice_dynamic-update-slice_fusion.4
  305.0 6.6 %fusion.39 = f32[1024,256]{1,0:T(8,128)S(1)} fusion(bf16[256,4096]{1,0:T(8,128)(2,1)} %collective-permute-done.3, bf16[512,4096]{1,0:T(8,128)(2,1)} %get-tuple-element.46, bf16[512,4096]{1,0:T(8,128)(2,1)} %get-tuple-element.44), kind=kOutput, calls=%fused_computation.110 | convolution fusion | flops 2164260864 | bytes 11534336 | tf_op jit(solution)/shard_map/dot_general | solution.py:19
  311.7 1.3 fusion.12
  313.9 6.7 %fusion.38 = f32[1024,128]{0,1:T(8,128)S(1)} fusion(bf16[128,4096]{1,0:T(8,128)(2,1)} %collective-permute-done.4, bf16[512,4096]{1,0:T(8,128)(2,1)} %get-tuple-element.46, bf16[512,4096]{1,0:T(8,128)(2,1)} %get-tuple-element.44), kind=kOutput, calls=%fused_computation.109 | convolution fusion | flops 1090519040 | bytes 9961472 | tf_op jit(solution)/shard_map/dot_general | solution.py:19
  320.7 1.3 fusion.24
  322.8 46.4 %all-reduce.16.cloned.1.call-done = f32[512,256]{0,1:T(8,128)} async-done(((f32[512,256]{0,1:T(8,128)}), f32[512,256]{0,1:T(8,128)}) %all-reduce.16.cloned.1.call-update) | async-done | bytes 524304 | tf_op jit(solution)/shard_map/psum | solution.py:90
  369.2 1.0 slice_dynamic-update-slice_fusion.3
  370.2 55.2 %all-reduce.18.cloned.1.call-done = f32[512,128]{0,1:T(8,128)} async-done(((f32[512,128]{0,1:T(8,128)}), f32[512,128]{0,1:T(8,128)}) %all-reduce.18.cloned.1.call-update) | async-done | bytes 262160 | tf_op jit(solution)/shard_map/psum | solution.py:90
  425.3 0.9 slice_dynamic-update-slice_fusion.8
  426.3 1.0 slice_dynamic-update-slice_fusion.2
  427.2 1.0 slice_dynamic-update-slice_fusion.1
  428.2 1.0 slice_dynamic-update-slice_fusion
  429.2 0.9 slice_dynamic-update-slice_fusion.6
  431.4 1.0 fusion.48
  433.4 1.5 collective-permute-start.6
  435.1 1.0 fusion.49
  436.4 1.6 collective-permute-start.7
  438.0 34.0 %collective-permute-done.7 = f32[2,64,512]{1,2,0:T(8,128)} collective-permute-done((f32[2,64,512]{1,2,0:T(8,128)S(1)}, f32[2,64,512]{1,2,0:T(8,128)}, u32[]{:S(2)}, u32[]{:S(2)}) %collective-permute-start.7) | collective-permute-done | bytes 262176 | tf_op jit(solution)/shard_map/ppermute | solution.py:102
  472.0 1.1 broadcast_select_fusion.1
  473.3 1.2 fusion.51
  474.9 1.2 fusion.50
  476.2 1.2 copy.23
  (94 shorter events, 9.6 us)
Async XLA Ops:
  6.5 123.1 %all-reduce.8.cloned.1.call-start = ((), (), s32[]{:S(2)}) async-start(), calls=%async_computation | async-start | bytes 4194304 | tf_op jit(solution)/shard_map/psum | solution.py:69
  8.3 27.0 %collective-permute-start = (bf16[128,4096]{1,0:T(8,128)(2,1)S(1)}, bf16[128,4096]{1,0:T(8,128)(2,1)S(1)}, u32[]{:S(2)}, u32[]{:S(2)}) collective-permute-start(bf16[128,4096]{1,0:T(8,128)(2,1)S(1)} %pad_maximum_fusion.5), channel_id=1, source_target_pairs={{0,24},{8,0},{16,8},{24,16},{1,25},{9,1},{17,9},{25,17},{2,26},{10... | collective-permute-start | bytes 3145736 | tf_op jit(solution)/shard_map/ppermute | solution.py:62
  8.9 26.4 %slice-start = ((s8[8388608]{0:T(1024)(128)(4,1)}), s8[4194304]{0:T(1024)(128)(4,1)S(1)}, s32[]{:S(2)}) async-start(s8[8388608]{0:T(1024)(128)(4,1)} %bitcast.72), calls=%async_computation.6 | async-start | bytes 8388608
  12.3 23.0 %slice-start.1 = ((s8[8388608]{0:T(1024)(128)(4,1)}), s8[4194304]{0:T(1024)(128)(4,1)S(1)}, s32[]{:S(2)}) async-start(s8[8388608]{0:T(1024)(128)(4,1)} %bitcast.72), calls=%async_computation.7 | async-start | bytes 8388608
  13.7 115.8 %collective-permute-start.1 = (bf16[256,4096]{1,0:T(8,128)(2,1)}, bf16[256,4096]{1,0:T(8,128)(2,1)}, u32[]{:S(2)}, u32[]{:S(2)}) collective-permute-start(bf16[256,4096]{1,0:T(8,128)(2,1)} %pad_maximum_fusion.2), channel_id=1, source_target_pairs={{0,24},{8,0},{16,8},{24,16},{1,25},{9,1},{17,9},{25,17},{2,26},{10... | collective-permute-start | bytes 6291464 | tf_op jit(solution)/shard_map/ppermute | solution.py:62
  15.4 23.5 %slice-start.2 = ((s8[8388608]{0:T(1024)(128)(4,1)}), s8[4194304]{0:T(1024)(128)(4,1)S(1)}, s32[]{:S(2)}) async-start(s8[8388608]{0:T(1024)(128)(4,1)} %bitcast.74), calls=%async_computation.8 | async-start | bytes 8388608
  16.9 22.0 %slice-start.3 = ((s8[8388608]{0:T(1024)(128)(4,1)}), s8[4194304]{0:T(1024)(128)(4,1)S(1)}, s32[]{:S(2)}) async-start(s8[8388608]{0:T(1024)(128)(4,1)} %bitcast.74), calls=%async_computation.9 | async-start | bytes 8388608
  35.3 3.6 copy-start.12
  63.2 125.9 %all-reduce.10.cloned.1.call-start = ((), (), s32[]{:S(2)}) async-start(), calls=%async_computation.1 | async-start | bytes 524288 | tf_op jit(solution)/shard_map/psum | solution.py:90
  64.4 124.9 %collective-permute-start.2 = (bf16[256,4096]{1,0:T(8,128)(2,1)S(1)}, bf16[256,4096]{1,0:T(8,128)(2,1)}, u32[]{:S(2)}, u32[]{:S(2)}) collective-permute-start(bf16[256,4096]{1,0:T(8,128)(2,1)S(1)} %pad_maximum_fusion.3), channel_id=1, source_target_pairs={{0,24},{8,0},{16,8},{24,16},{1,25},{9,1},{17,9},{25,17},{2,26},{10... | collective-permute-start | bytes 6291464 | tf_op jit(solution)/shard_map/ppermute | solution.py:62
  131.4 1.0 copy-start.1
  131.4 2.3 copy-start.6
  134.5 112.2 %all-reduce.12.cloned.1.call-start = ((), (), s32[]{:S(2)}) async-start(), calls=%async_computation.2 | async-start | bytes 1048576 | tf_op jit(solution)/shard_map/psum | solution.py:90
  134.6 6.7 %copy-start.2 = (f32[512,512]{0,1:T(8,128)S(1)}, f32[512,512]{0,1:T(8,128)}, u32[]{:S(2)}) copy-start(f32[512,512]{0,1:T(8,128)} %copy-done.1) | copy-start | bytes 3145732
  134.6 6.7 %copy-start.7 = (f32[512,512]{0,1:T(8,128)S(1)}, f32[512,512]{0,1:T(8,128)}, u32[]{:S(2)}) copy-start(f32[512,512]{0,1:T(8,128)} %copy-done.6) | copy-start | bytes 3145732
  142.6 162.4 %collective-permute-start.3 = (bf16[256,4096]{1,0:T(8,128)(2,1)}, bf16[256,4096]{1,0:T(8,128)(2,1)}, u32[]{:S(2)}, u32[]{:S(2)}) collective-permute-start(bf16[256,4096]{1,0:T(8,128)(2,1)} %pad_maximum_fusion.4), channel_id=1, source_target_pairs={{0,24},{8,0},{16,8},{24,16},{1,25},{9,1},{17,9},{25,17},{2,26},{10... | collective-permute-start | bytes 6291464 | tf_op jit(solution)/shard_map/ppermute | solution.py:62
  189.2 114.9 %all-reduce.14.cloned.1.call-start = ((), (), s32[]{:S(2)}) async-start(), calls=%async_computation.3 | async-start | bytes 1048576 | tf_op jit(solution)/shard_map/psum | solution.py:90
  189.2 6.7 %copy-start.3 = (f32[512,512]{0,1:T(8,128)S(1)}, f32[512,512]{0,1:T(8,128)}, u32[]{:S(2)}) copy-start(f32[512,512]{0,1:T(8,128)} %copy-done.1) | copy-start | bytes 3145732
  189.2 6.7 %copy-start.8 = (f32[512,512]{0,1:T(8,128)S(1)}, f32[512,512]{0,1:T(8,128)}, u32[]{:S(2)}) copy-start(f32[512,512]{0,1:T(8,128)} %copy-done.6) | copy-start | bytes 3145732
  195.9 50.9 %copy-start.11 = (f32[512,128]{0,1:T(8,128)S(1)}, f32[512,128]{0,1:T(8,128)}, u32[]{:S(2)}) copy-start(f32[512,128]{0,1:T(8,128)} %all-reduce.10.cloned.1.call-done) | copy-start | bytes 786436
  246.8 122.4 %all-reduce.16.cloned.1.call-start = ((), (), s32[]{:S(2)}) async-start(), calls=%async_computation.4 | async-start | bytes 1048576 | tf_op jit(solution)/shard_map/psum | solution.py:90
  247.8 66.1 %collective-permute-start.4 = (bf16[128,4096]{1,0:T(8,128)(2,1)}, bf16[128,4096]{1,0:T(8,128)(2,1)}, u32[]{:S(2)}, u32[]{:S(2)}) collective-permute-start(bf16[128,4096]{1,0:T(8,128)(2,1)} %pad_maximum_fusion.6), channel_id=1, source_target_pairs={{0,24},{8,0},{16,8},{24,16},{1,25},{9,1},{17,9},{25,17},{2,26},{10... | collective-permute-start | bytes 3145736 | tf_op jit(solution)/shard_map/ppermute | solution.py:62
  305.0 6.7 %copy-start.4 = (f32[512,512]{0,1:T(8,128)S(1)}, f32[512,512]{0,1:T(8,128)}, u32[]{:S(2)}) copy-start(f32[512,512]{0,1:T(8,128)} %copy-done.1) | copy-start | bytes 3145732
  305.0 6.7 %copy-start.9 = (f32[512,512]{0,1:T(8,128)S(1)}, f32[512,512]{0,1:T(8,128)}, u32[]{:S(2)}) copy-start(f32[512,512]{0,1:T(8,128)} %copy-done.6) | copy-start | bytes 3145732
  313.9 111.5 %all-reduce.18.cloned.1.call-start = ((), (), s32[]{:S(2)}) async-start(), calls=%async_computation.5 | async-start | bytes 524288 | tf_op jit(solution)/shard_map/psum | solution.py:90
  313.9 6.8 %copy-start.5 = (f32[512,512]{0,1:T(8,128)S(1)}, f32[512,512]{0,1:T(8,128)}, u32[]{:S(2)}) copy-start(f32[512,512]{0,1:T(8,128)} %copy-done.1) | copy-start | bytes 3145732
  313.9 6.8 %copy-start.10 = (f32[512,512]{0,1:T(8,128)S(1)}, f32[512,512]{0,1:T(8,128)}, u32[]{:S(2)}) copy-start(f32[512,512]{0,1:T(8,128)} %copy-done.6) | copy-start | bytes 3145732
  430.4 0.8 collective-permute-start.5
  433.4 1.5 collective-permute-start.6
  436.4 35.6 %collective-permute-start.7 = (f32[2,64,512]{1,2,0:T(8,128)S(1)}, f32[2,64,512]{1,2,0:T(8,128)}, u32[]{:S(2)}, u32[]{:S(2)}) collective-permute-start(f32[2,64,512]{1,2,0:T(8,128)S(1)} %pad_maximum_fusion.12), channel_id=1, source_target_pairs={{16,24},{17,25},{18,26},{19,27},{20,28},{21,29},{22,30},{23,31}} | collective-permute-start | bytes 786440 | tf_op jit(solution)/shard_map/ppermute | solution.py:102
  473.3 1.6 copy-start
Sparse Core Ops, SparseCore 0:
  63.4 66.1 all-reduce.7
  134.7 54.4 all-reduce.9
  191.6 55.0 all-reduce.11
  248.9 55.0 all-reduce.13
  314.0 55.1 all-reduce.15
  371.3 53.9 all-reduce.17
where the time goes:
time: 485 us; the launch traced here: 484 us
  waiting for transfers between devices  362 us (75%)
  matrix products  60.5 us (12%)
  local copies, waits for them, and re-layouts  23.3 us (5%)
  other arithmetic  17.2 us (4%)
  between operations  14.1 us (3%)
  starting transfers between devices  7.37 us (2%)
    psum x5, waiting for transfers between devices, shards(): sections.append(lax.psum(section, 'pw'))  251 us
    psum x1, waiting for transfers between devices, shards(): lax.psum(jnp.concatenate(margin_of(whole[k], whole[k + 1]), 1), 'pw')  58.6 us
    dot_general x6, matrix products, margin_of(): lax.dot_general(own, other, (((1,), (1,)), ((), ())), preferred_element_t...  49.6 us
    ppermute x3, waiting for transfers between devices, shards(): received = lax.ppermute(line, 'ka', [(place - 1, place)])  34.1 us
    ppermute x5, waiting for transfers between devices, shards(): arrivals.append(lax.ppermute(block, 'ka', to_previous))  18.4 us
    squeeze x4, local copies, waits for them, and re-layouts, packed(): parts = [s[kpoint, first:first + width] for s in (states_re, states_im)]  12.2 us
    dot_general x9, matrix products, exact_dot(): jnp.dot(left, right, precision=lax.Precision.HIGH, preferred_element_type...  10.8 us
  transfers between devices with their start and end apart: 14, of which 8 were waited for; matrix products, arithmetic and copies ran while one was open for 17% of the time, Pallas kernels for 0%

commit v1 on v0

--- a/solution.py
+++ b/solution.py
@@ -30,16 +30,62 @@
     )
 
 
-def rows_times(rows, matrix):
+def rows_times(rows, pieces):
     _, count, bands = rows.shape
-    dots = exact_dot(rows.reshape(2 * count, bands), matrix)
-    real_part = dots[:count, :bands] - dots[count:, bands:]
-    imag_part = dots[:count, bands:] + dots[count:, :bands]
-    return jnp.stack([real_part, imag_part], 0)
+    flat = rows.reshape(2 * count, bands)
+    reals, imags = [], []
+    for piece in pieces:
+        width = piece.shape[1] // 2
+        dots = exact_dot(flat, piece)
+        reals.append(dots[:count, :width] - dots[count:, width:])
+        imags.append(dots[:count, width:] + dots[count:, :width])
+    return jnp.stack([jnp.concatenate(reals, 1), jnp.concatenate(imags, 1)], 0)
 
 
 def after(value, earlier):
     return lax.optimization_barrier((value, earlier))[0]
+
+
+def other_core(block):
+    size = lax.axis_size("pw")
+    return lax.ppermute(block, "pw", [(i, i ^ 1) for i in range(size)])
+
+
+def other_chip(block, distance):
+    size = lax.axis_size("pw")
+    return lax.ppermute(block, "pw", [(i, (i + 2 * distance) % size) for i in range(size)])
+
+
+def take(blocks, place, axis):
+    return lax.dynamic_index_in_dim(blocks, place, axis, keepdims=False)
+
+
+def chosen(place, blocks):
+    picked = blocks[0]
+    for number, block in enumerate(blocks[1:], 1):
+        picked = jnp.where(place == number, block, picked)
+    return picked
+
+
+def sum_to_rows(part):
+    chips = lax.axis_size("pw") // 2
+    chip, core = lax.axis_index("pw") // 2, lax.axis_index("pw") % 2
+    blocks = part.reshape(chips, 2, part.shape[0] // (2 * chips), part.shape[1])
+    half = take(blocks, core, 1) + other_core(take(blocks, 1 - core, 1))
+    total = take(half, chip, 0)
+    received = [other_chip(take(half, (chip + d) % chips, 0), d) for d in range(1, chips)]
+    return sum(received, total)
+
+
+def rows_to_whole(rows):
+    chips = lax.axis_size("pw") // 2
+    chip, core = lax.axis_index("pw") // 2, lax.axis_index("pw") % 2
+    ring = [rows] + [other_chip(rows, d) for d in range(1, chips)]
+    mine = jnp.stack([chosen((chip - place) % chips, ring) for place in range(chips)], 0)
+    theirs = other_core(mine)
+    first = jnp.where(core == 0, mine, theirs)
+    second = jnp.where(core == 0, theirs, mine)
+    return jnp.stack([first, second], 1).reshape(-1, rows.shape[1])
 
 
 def shards(states_re, states_im):
@@ -50,8 +96,10 @@
     ka_place = lax.axis_index("ka")
     first_band = lax.axis_index("pw") * band_rows
     eighth = bands // 8
-    widths = [eighth, 2 * eighth, 2 * eighth, 2 * eighth, eighth]
+    little = bands // 32
+    widths = [little, 2 * eighth - little, 2 * eighth, 2 * eighth, 2 * eighth]
     firsts = [sum(widths[:i]) for i in range(len(widths))]
+    members = [[0, 1, 2, 3], [4]]
 
     to_previous = [(i, (i - 1) % ka_width) for i in range(ka_width)]
     arrivals = []
@@ -68,7 +116,7 @@
     for k in range(kcount - 1):
         margin = lax.psum(jnp.concatenate(margin_of(whole[k], whole[k + 1]), 1), "pw")
         if before is not None:
-            before = rows_times(jnp.stack([before[:, :bands], before[:, bands:]]), margin)
+            before = rows_times(jnp.stack([before[:, :bands], before[:, bands:]]), [margin])
             margin = jnp.concatenate([before[0], before[1]], 1)
         before = margin
         own_margins.append(margin)
@@ -76,24 +124,34 @@
 
     sections = []
     last_dots = None
-    for block in arrivals:
-        if last_dots is not None:
-            block = after(block, last_dots)
-        real_part, imag_part = margin_of(whole[kcount - 1], block)
-        last_dots = real_part
+    for group in members:
+        parts = []
+        for number in group:
+            block = arrivals[number]
+            if last_dots is not None:
+                block = after(block, last_dots)
+            parts.append(margin_of(whole[kcount - 1], block))
+            last_dots = parts[-1][0]
+        real_part, imag_part = (jnp.concatenate([p[i] for p in parts], 1) for i in (0, 1))
         if left is not None:
             product = exact_dot(left, jnp.concatenate([real_part, imag_part], 0))
             real_part, imag_part = product[:bands], product[bands:]
         section = jnp.concatenate([real_part, imag_part], 1)
-        if sections:
-            section = after(section, sections[-1])
-        sections.append(lax.psum(section, "pw"))
-    reals = [section[:, : section.shape[1] // 2] for section in sections]
-    imags = [section[:, section.shape[1] // 2 :] for section in sections]
-    span = jnp.concatenate(reals + imags, 1)
+        if number < len(widths) - 1:
+            whole_section = lax.psum(section, "pw")
+            rows = lax.dynamic_slice_in_dim(whole_section, first_band, band_rows, 0)
+        else:
+            rows = sum_to_rows(section)
+            whole_section = rows_to_whole(rows)
+        sections.append((rows, whole_section))
+    spans = [whole_section for _, whole_section in sections]
 
-    line = lax.dynamic_slice_in_dim(span, first_band, band_rows, 0)
-    line = jnp.stack([line[:, :bands], line[:, bands:]], 0)
+    reals, imags = [], []
+    for rows, _ in sections:
+        width = rows.shape[1] // 2
+        reals.append(rows[:, :width])
+        imags.append(rows[:, width:])
+    line = jnp.stack([jnp.concatenate(reals, 1), jnp.concatenate(imags, 1)], 0)
     row_index = lax.broadcasted_iota(jnp.int32, (band_rows, bands), 0) + first_band
     col_index = lax.broadcasted_iota(jnp.int32, (band_rows, bands), 1)
     eye_real = (row_index == col_index).astype(jnp.float32)
@@ -102,9 +160,9 @@
         received = lax.ppermute(line, "ka", [(place - 1, place)])
         start = jnp.where(ka_place == place, received, start)
         if place < ka_width - 1:
-            line = rows_times(start, span)
+            line = rows_times(start, spans)
 
-    lines = [rows_times(start, matrix) for matrix in own_margins + [span]]
+    lines = [rows_times(start, [margin]) for margin in own_margins] + [rows_times(start, spans)]
     return jnp.stack([jnp.moveaxis(one, 0, 1) for one in lines], 0)
 
 

time: 485 us -> 307 us (0.63)
  waiting for transfers between devices: 362 us -> 189 us
  matrix products: 60.5 us -> 50.5 us
  starting transfers between devices: 7.37 us -> 12.7 us
    psum x5 -> x1, waiting for transfers between devices: 251 us -> 20.7 us  [shards(): whole_section = lax.psum(section, 'pw')]
    ppermute x5, waiting for transfers between devices: 18.4 us -> 70.2 us  [shards(): arrivals.append(lax.ppermute(block, 'ka', to_previous))]
    ppermute x0 -> x8, waiting for transfers between devices: none -> 10.2 us  [the longest x6 8.95 us: other_chip(): lax.ppermute(block, 'pw', [(i, (i + 2 * distance) % size) for i in range(...]
    dot_general x6, matrix products: 49.6 us -> 41.3 us  [margin_of(): lax.dot_general(own, other, (((1,), (1,)), ((), ())), preferred_element_t...]
    ppermute x0 -> x8, starting transfers between devices: none -> 6.1 us  [the longest x6 6.03 us: other_chip(): lax.ppermute(block, 'pw', [(i, (i + 2 * distance) % size) for i in range(...]
    ppermute x3, waiting for transfers between devices: 34.1 us -> 28.4 us  [shards(): received = lax.ppermute(line, 'ka', [(place - 1, place)])]
    squeeze x4 -> x5, local copies, waits for them, and re-layouts: 12.2 us -> 13.6 us  [packed(): parts = [s[kpoint, first:first + width] for s in (states_re, states_im)]]
  transfers between devices with their start and end apart: 14 -> 18, of which waited for: 8 -> 8; matrix products, arithmetic and copies ran while one was open for 17% -> 24% of each run, Pallas kernels for 0% -> 0%
where the time goes in v1:
time: 307 us
  waiting for transfers between devices  189 us (62%)
  matrix products  50.5 us (16%)
  local copies, waits for them, and re-layouts  21.9 us (7%)
  other arithmetic  18.1 us (6%)
  between operations  14.3 us (5%)
  starting transfers between devices  12.7 us (4%)
    ppermute x5, waiting for transfers between devices, shards(): arrivals.append(lax.ppermute(block, 'ka', to_previous))  70.2 us
    psum x1, waiting for transfers between devices, shards(): lax.psum(jnp.concatenate(margin_of(whole[k], whole[k + 1]), 1), 'pw')  59.7 us
    dot_general x6, matrix products, margin_of(): lax.dot_general(own, other, (((1,), (1,)), ((), ())), preferred_element_t...  41.3 us
    ppermute x3, waiting for transfers between devices, shards(): received = lax.ppermute(line, 'ka', [(place - 1, place)])  28.4 us
    psum x1, waiting for transfers between devices, shards(): whole_section = lax.psum(section, 'pw')  20.7 us
    squeeze x5, local copies, waits for them, and re-layouts, packed(): parts = [s[kpoint, first:first + width] for s in (states_re, states_im)]  13.6 us
    dot_general x9, matrix products, exact_dot(): jnp.dot(left, right, precision=lax.Precision.HIGH, preferred_element_type...  9.26 us
    ppermute x6, waiting for transfers between devices, other_chip(): lax.ppermute(block, 'pw', [(i, (i + 2 * distance) % size) for i in range(...  8.95 us
  transfers between devices with their start and end apart: 18, of which 8 were waited for; matrix products, arithmetic and copies ran while one was open for 24% of the time, Pallas kernels for 0%

profile of v1, /device:TPU:6, one launch (start us, length us, event | category | flops | bytes accessed | tf_op | source)
XLA Modules:
  0.0 306.9 jit_solution(8560928857323776521)
XLA Ops:
  6.5 1.1 slice_bitcast_fusion.12
  8.3 2.0 slice_bitcast_fusion.10
  10.3 1.4 pad_maximum_fusion.5
  11.7 1.0 collective-permute-start.1
  12.7 2.5 slice_bitcast_fusion.6
  15.2 1.5 pad_maximum_fusion.4
  16.6 1.5 pad_maximum_fusion.2
  18.2 4.4 %slice_bitcast_fusion = (bf16[512,4096]{1,0:T(8,128)(2,1)}, bf16[512,4096]{1,0:T(8,128)(2,1)}) fusion(bf16[2,512,4096]{2,1,0:T(8,128)(2,1)S(1)} %copy-done), kind=kLoop, calls=%fused_computation.6 | loop fusion | bytes 16777216 | tf_op jit(solution)/shard_map/squeeze | solution.py:12
  22.6 1.4 slice-done.1
  24.0 3.5 %slice_bitcast_fusion.1 = (bf16[512,4096]{1,0:T(8,128)(2,1)}, bf16[512,4096]{1,0:T(8,128)(2,1)}) fusion(bf16[2,512,4096]{2,1,0:T(8,128)(2,1)S(1)} %bitcast.106), kind=kLoop, calls=%fused_computation.7 | loop fusion | bytes 16777216 | tf_op jit(solution)/shard_map/squeeze | solution.py:12
  27.5 16.7 %fusion = f32[1024,1024]{0,1:T(8,128)} fusion(bf16[512,4096]{1,0:T(8,128)(2,1)} %get-tuple-element.34, bf16[512,4096]{1,0:T(8,128)(2,1)} %get-tuple-element.32, bf16[512,4096]{1,0:T(8,128)(2,1)} %get-tuple-element.33, bf16[512,4096]{1,0:T(8,128)(2,1)} %get-tuple-element.31), kind=kOutput, calls=%fused_computation | convolution fusion | flops 8623489024 | bytes 20971520 | tf_op jit(solution)/shard_map/dot_general | solution.py:19
  44.2 2.6 slice_add_fusion
  46.8 1.5 pad_maximum_fusion.1
  48.7 1.5 pad_maximum_fusion.3
  50.2 4.9 %fusion.35 = f32[1024,32]{0,1:T(8,128)S(1)} fusion(bf16[32,4096]{1,0:T(8,128)(2,1)S(1)} %collective-permute-done, bf16[512,4096]{1,0:T(8,128)(2,1)} %get-tuple-element.33, bf16[512,4096]{1,0:T(8,128)(2,1)} %get-tuple-element.31), kind=kOutput, calls=%fused_computation.121 | convolution fusion | flops 285212672 | bytes 8781824 | tf_op jit(solution)/shard_map/dot_general | solution.py:19
  55.2 59.7 %all-reduce.4.cloned.1.call-done = f32[512,1024]{0,1:T(8,128)} async-done(((f32[512,1024]{0,1:T(8,128)}), f32[512,1024]{0,1:T(8,128)}) %all-reduce.4.cloned.1.call-update) | async-done | bytes 2097168 | tf_op jit(solution)/shard_map/psum | solution.py:117
  115.4 6.8 %fusion.34 = f32[1024,224]{0,1:T(8,128)S(1)} fusion(bf16[224,4096]{1,0:T(8,128)(2,1)} %collective-permute-done.1, bf16[512,4096]{1,0:T(8,128)(2,1)} %get-tuple-element.33, bf16[512,4096]{1,0:T(8,128)(2,1)} %get-tuple-element.31), kind=kOutput, calls=%fused_computation.120 | convolution fusion | flops 1895825408 | bytes 11141120 | tf_op jit(solution)/shard_map/dot_general | solution.py:19
  122.6 1.6 copy-done.6
  124.2 1.5 collective-permute-start.4
  125.7 4.0 %fusion.33 = f32[1024,256]{0,1:T(8,128)S(1)} fusion(bf16[256,4096]{1,0:T(8,128)(2,1)} %collective-permute-done.2, bf16[512,4096]{1,0:T(8,128)(2,1)S(1)} %copy-done.4, bf16[512,4096]{1,0:T(8,128)(2,1)S(1)} %copy-done.5), kind=kOutput, calls=%fused_computation.119 | convolution fusion | flops 2164260864 | bytes 11534336 | tf_op jit(solution)/shard_map/dot_general | solution.py:19
  129.8 34.7 %collective-permute-done.3 = bf16[256,4096]{1,0:T(8,128)(2,1)S(1)} collective-permute-done((bf16[256,4096]{1,0:T(8,128)(2,1)}, bf16[256,4096]{1,0:T(8,128)(2,1)S(1)}, u32[]{:S(2)}, u32[]{:S(2)}) %collective-permute-start.3) | collective-permute-done | bytes 2097184 | tf_op jit(solution)/shard_map/ppermute | solution.py:110
  164.5 2.4 fusion.32
  167.0 2.8 fusion.5
  170.0 1.3 pad_maximum_fusion.6
  171.3 35.5 %collective-permute-done.4 = bf16[256,4096]{1,0:T(8,128)(2,1)} collective-permute-done((bf16[256,4096]{1,0:T(8,128)(2,1)S(1)}, bf16[256,4096]{1,0:T(8,128)(2,1)}, u32[]{:S(2)}, u32[]{:S(2)}) %collective-permute-start.4) | collective-permute-done | bytes 2097184 | tf_op jit(solution)/shard_map/ppermute | solution.py:110
  206.8 6.6 %fusion.31 = f32[1024,256]{1,0:T(8,128)S(1)} fusion(bf16[256,4096]{1,0:T(8,128)(2,1)} %collective-permute-done.4, bf16[512,4096]{1,0:T(8,128)(2,1)} %get-tuple-element.33, bf16[512,4096]{1,0:T(8,128)(2,1)} %get-tuple-element.31), kind=kOutput, calls=%fused_computation.117 | convolution fusion | flops 2164260864 | bytes 11534336 | tf_op jit(solution)/shard_map/dot_general | solution.py:19
  213.5 1.3 fusion.4
  215.5 1.3 collective-permute-done.5
  217.1 1.8 collective-permute-start.8
  219.5 0.8 collective-permute-start.6
  220.4 20.7 %all-reduce.6.cloned.1.call-done = f32[512,768]{0,1:T(8,128)} async-done(((f32[512,768]{0,1:T(8,128)}), f32[512,768]{0,1:T(8,128)}) %all-reduce.6.cloned.1.call-update) | async-done | bytes 1572880 | tf_op jit(solution)/shard_map/psum | solution.py:141
  241.1 1.3 constant_dynamic-slice_fusion
  242.5 2.1 collective-permute-start.10
  246.4 1.7 collective-permute-done.10
  248.1 7.2 %collective-permute-done.11 = f32[64,256]{0,1:T(8,128)S(1)} collective-permute-done((f32[64,256]{0,1:T(8,128)S(1)}, f32[64,256]{0,1:T(8,128)S(1)}, u32[]{:S(2)}, u32[]{:S(2)}) %collective-permute-start.11) | collective-permute-done | bytes 65568 | tf_op jit(solution)/shard_map/ppermute | solution.py:56
  255.4 0.8 pad_maximum_fusion.10
  256.2 0.8 copy-done.7
  257.3 0.8 fusion.39
  258.1 0.9 slice_subtract_fusion.6
  260.2 0.9 maximum_bitcast_fusion.3
  261.1 0.9 maximum_bitcast_fusion.2
  263.8 0.8 fusion.41
  264.9 1.3 collective-permute-start.15
  266.2 28.4 %collective-permute-done.15 = f32[2,64,512]{1,2,0:T(8,128)} collective-permute-done((f32[2,64,512]{1,2,0:T(8,128)S(1)}, f32[2,64,512]{1,2,0:T(8,128)}, u32[]{:S(2)}, u32[]{:S(2)}) %collective-permute-start.15) | collective-permute-done | bytes 262176 | tf_op jit(solution)/shard_map/ppermute | solution.py:160
  294.6 1.1 broadcast_select_fusion.1
  296.2 0.9 fusion.44
  297.5 1.2 fusion.43
  298.8 1.2 copy.69
  (102 shorter events, 10.0 us)
Async XLA Ops:
  6.5 108.3 %all-reduce.4.cloned.1.call-start = ((), (), s32[]{:S(2)}) async-start(), calls=%async_computation | async-start | bytes 4194304 | tf_op jit(solution)/shard_map/psum | solution.py:117
  6.5 6.1 %copy-start = (bf16[2,512,4096]{2,1,0:T(8,128)(2,1)S(1)}, bf16[2,512,4096]{2,1,0:T(8,128)(2,1)}, u32[]{:S(2)}) copy-start(bf16[2,512,4096]{2,1,0:T(8,128)(2,1)} %param.3) | copy-start | bytes 25165828
  7.7 10.5 %collective-permute-start = (bf16[32,4096]{1,0:T(8,128)(2,1)S(1)}, bf16[32,4096]{1,0:T(8,128)(2,1)S(1)}, u32[]{:S(2)}, u32[]{:S(2)}) collective-permute-start(bf16[32,4096]{1,0:T(8,128)(2,1)S(1)} %pad_maximum_fusion.14), channel_id=1, source_target_pairs={{0,24},{8,0},{16,8},{24,16},{1,25},{9,1},{17,9},{25,17},{2,26},{10... | collective-permute-start | bytes 786440 | tf_op jit(solution)/shard_map/ppermute | solution.py:110
  11.7 103.2 %collective-permute-start.1 = (bf16[224,4096]{1,0:T(8,128)(2,1)}, bf16[224,4096]{1,0:T(8,128)(2,1)}, u32[]{:S(2)}, u32[]{:S(2)}) collective-permute-start(bf16[224,4096]{1,0:T(8,128)(2,1)} %pad_maximum_fusion.5), channel_id=1, source_target_pairs={{0,24},{8,0},{16,8},{24,16},{1,25},{9,1},{17,9},{25,17},{2,26},{10... | collective-permute-start | bytes 5505032 | tf_op jit(solution)/shard_map/ppermute | solution.py:110
  16.6 5.9 %slice-start = ((s8[8388608]{0:T(1024)(128)(4,1)}), s8[4194304]{0:T(1024)(128)(4,1)S(1)}, s32[]{:S(2)}) async-start(s8[8388608]{0:T(1024)(128)(4,1)} %bitcast.105), calls=%async_computation.2 | async-start | bytes 8388608
  18.2 5.8 %slice-start.1 = ((s8[8388608]{0:T(1024)(128)(4,1)}), s8[4194304]{0:T(1024)(128)(4,1)S(1)}, s32[]{:S(2)}) async-start(s8[8388608]{0:T(1024)(128)(4,1)} %bitcast.105), calls=%async_computation.3 | async-start | bytes 8388608
  48.3 192.8 %all-reduce.6.cloned.1.call-start = ((), (), s32[]{:S(2)}) async-start(), calls=%async_computation.1 | async-start | bytes 3145728 | tf_op jit(solution)/shard_map/psum | solution.py:141
  48.4 74.2 %collective-permute-start.2 = (bf16[256,4096]{1,0:T(8,128)(2,1)}, bf16[256,4096]{1,0:T(8,128)(2,1)}, u32[]{:S(2)}, u32[]{:S(2)}) collective-permute-start(bf16[256,4096]{1,0:T(8,128)(2,1)} %pad_maximum_fusion.2), channel_id=1, source_target_pairs={{0,24},{8,0},{16,8},{24,16},{1,25},{9,1},{17,9},{25,17},{2,26},{10... | collective-permute-start | bytes 6291464 | tf_op jit(solution)/shard_map/ppermute | solution.py:110
  114.9 49.7 %collective-permute-start.3 = (bf16[256,4096]{1,0:T(8,128)(2,1)}, bf16[256,4096]{1,0:T(8,128)(2,1)S(1)}, u32[]{:S(2)}, u32[]{:S(2)}) collective-permute-start(bf16[256,4096]{1,0:T(8,128)(2,1)} %pad_maximum_fusion.3), channel_id=1, source_target_pairs={{0,24},{8,0},{16,8},{24,16},{1,25},{9,1},{17,9},{25,17},{2,26},{10... | collective-permute-start | bytes 6291464 | tf_op jit(solution)/shard_map/ppermute | solution.py:110
  115.4 6.9 %copy-start.2 = (f32[512,1024]{0,1:T(8,128)S(1)}, f32[512,1024]{0,1:T(8,128)}, u32[]{:S(2)}) copy-start(f32[512,1024]{0,1:T(8,128)} %all-reduce.4.cloned.1.call-done) | copy-start | bytes 6291460
  115.4 10.3 %copy-start.5 = (bf16[512,4096]{1,0:T(8,128)(2,1)S(1)}, bf16[512,4096]{1,0:T(8,128)(2,1)}, u32[]{:S(2)}) copy-start(bf16[512,4096]{1,0:T(8,128)(2,1)} %get-tuple-element.31) | copy-start | bytes 12582916
  122.2 2.0 copy-start.6
  122.2 3.6 %copy-start.4 = (bf16[512,4096]{1,0:T(8,128)(2,1)S(1)}, bf16[512,4096]{1,0:T(8,128)(2,1)}, u32[]{:S(2)}) copy-start(bf16[512,4096]{1,0:T(8,128)(2,1)} %get-tuple-element.33) | copy-start | bytes 12582916
  122.6 44.4 %copy-start.8 = (f32[512,512]{0,1:T(8,128)}, f32[512,512]{0,1:T(8,128)S(1)}, u32[]{:S(2)}) copy-start(f32[512,512]{0,1:T(8,128)S(1)} %get-tuple-element.38) | copy-start | bytes 3145732
  122.6 44.4 %copy-start.10 = (f32[512,512]{0,1:T(8,128)}, f32[512,512]{0,1:T(8,128)S(1)}, u32[]{:S(2)}) copy-start(f32[512,512]{0,1:T(8,128)S(1)} %get-tuple-element.39) | copy-start | bytes 3145732
  124.2 82.6 %collective-permute-start.4 = (bf16[256,4096]{1,0:T(8,128)(2,1)S(1)}, bf16[256,4096]{1,0:T(8,128)(2,1)}, u32[]{:S(2)}, u32[]{:S(2)}) collective-permute-start(bf16[256,4096]{1,0:T(8,128)(2,1)S(1)} %copy-done.6), channel_id=1, source_target_pairs={{0,24},{8,0},{16,8},{24,16},{1,25},{9,1},{17,9},{25,17},{2,26},{10... | collective-permute-start | bytes 6291464 | tf_op jit(solution)/shard_map/ppermute | solution.py:110
  171.3 42.2 %copy-start.9 = (f32[512,512]{0,1:T(8,128)S(1)}, f32[512,512]{0,1:T(8,128)}, u32[]{:S(2)}) copy-start(f32[512,512]{0,1:T(8,128)} %copy-done.8) | copy-start | bytes 3145732
  171.3 42.2 %copy-start.11 = (f32[512,512]{0,1:T(8,128)S(1)}, f32[512,512]{0,1:T(8,128)}, u32[]{:S(2)}) copy-start(f32[512,512]{0,1:T(8,128)} %copy-done.10) | copy-start | bytes 3145732
  215.1 1.6 collective-permute-start.5
  217.1 25.3 %collective-permute-start.8 = (f32[64,256]{0,1:T(8,128)S(1)}, f32[64,256]{0,1:T(8,128)S(1)}, u32[]{:S(2)}, u32[]{:S(2)}) collective-permute-start(f32[64,256]{0,1:T(8,128)S(1)} %bitcast.119), channel_id=1, source_target_pairs={{0,6},{1,7},{2,0},{3,1},{4,2},{5,3},{6,4},{7,5},{8,14},{9,15},{10,... | collective-permute-start | bytes 196616 | tf_op jit(solution)/shard_map/ppermute | solution.py:56
  219.0 23.4 %collective-permute-start.7 = (f32[64,256]{0,1:T(8,128)S(1)}, f32[64,256]{0,1:T(8,128)S(1)}, u32[]{:S(2)}, u32[]{:S(2)}) collective-permute-start(f32[64,256]{0,1:T(8,128)S(1)} %bitcast.120), channel_id=1, source_target_pairs={{0,4},{1,5},{2,6},{3,7},{4,0},{5,1},{6,2},{7,3},{8,12},{9,13},{10,... | collective-permute-start | bytes 196616 | tf_op jit(solution)/shard_map/ppermute | solution.py:56
  219.5 22.9 %collective-permute-start.6 = (f32[64,256]{0,1:T(8,128)S(1)}, f32[64,256]{0,1:T(8,128)S(1)}, u32[]{:S(2)}, u32[]{:S(2)}) collective-permute-start(f32[64,256]{0,1:T(8,128)S(1)} %bitcast.121), channel_id=1, source_target_pairs={{0,2},{1,3},{2,4},{3,5},{4,6},{5,7},{6,0},{7,1},{8,10},{9,11},{10,... | collective-permute-start | bytes 196616 | tf_op jit(solution)/shard_map/ppermute | solution.py:56
  241.1 16.1 %copy-start.1 = (f32[512,768]{0,1:T(8,128)S(1)}, f32[512,768]{0,1:T(8,128)}, u32[]{:S(2)}) copy-start(f32[512,768]{0,1:T(8,128)} %all-reduce.6.cloned.1.call-done) | copy-start | bytes 4718596
  242.5 5.6 %collective-permute-start.10 = (f32[64,256]{0,1:T(8,128)S(1)}, f32[64,256]{0,1:T(8,128)S(1)}, u32[]{:S(2)}, u32[]{:S(2)}) collective-permute-start(f32[64,256]{0,1:T(8,128)S(1)} %fusion.27), channel_id=1, source_target_pairs={{0,6},{1,7},{2,0},{3,1},{4,2},{5,3},{6,4},{7,5},{8,14},{9,15},{10,... | collective-permute-start | bytes 196616 | tf_op jit(solution)/shard_map/ppermute | solution.py:56
  244.6 10.7 %collective-permute-start.11 = (f32[64,256]{0,1:T(8,128)S(1)}, f32[64,256]{0,1:T(8,128)S(1)}, u32[]{:S(2)}, u32[]{:S(2)}) collective-permute-start(f32[64,256]{0,1:T(8,128)S(1)} %fusion.27), channel_id=1, source_target_pairs={{0,4},{1,5},{2,6},{3,7},{4,0},{5,1},{6,2},{7,3},{8,12},{9,13},{10,... | collective-permute-start | bytes 196616 | tf_op jit(solution)/shard_map/ppermute | solution.py:56
  245.2 10.1 %collective-permute-start.12 = (f32[64,256]{0,1:T(8,128)S(1)}, f32[64,256]{0,1:T(8,128)S(1)}, u32[]{:S(2)}, u32[]{:S(2)}) collective-permute-start(f32[64,256]{0,1:T(8,128)S(1)} %fusion.27), channel_id=1, source_target_pairs={{0,2},{1,3},{2,4},{3,5},{4,6},{5,7},{6,0},{7,1},{8,10},{9,11},{10,... | collective-permute-start | bytes 196616 | tf_op jit(solution)/shard_map/ppermute | solution.py:56
  245.7 10.6 %collective-permute-start.9 = (f32[2,64,512]{1,2,0:T(8,128)S(1)}, f32[2,64,512]{1,2,0:T(8,128)S(1)}, u32[]{:S(2)}, u32[]{:S(2)}) collective-permute-start(f32[2,64,512]{1,2,0:T(8,128)S(1)} %pad_maximum_fusion.9), channel_id=1, source_target_pairs={{0,8},{1,9},{2,10},{3,11},{4,12},{5,13},{6,14},{7,15}} | collective-permute-start | bytes 786440 | tf_op jit(solution)/shard_map/ppermute | solution.py:160
  256.2 2.8 collective-permute-start.13
  256.2 0.8 copy-start.7
  262.1 0.7 collective-permute-start.14
  264.9 29.7 %collective-permute-start.15 = (f32[2,64,512]{1,2,0:T(8,128)S(1)}, f32[2,64,512]{1,2,0:T(8,128)}, u32[]{:S(2)}, u32[]{:S(2)}) collective-permute-start(f32[2,64,512]{1,2,0:T(8,128)S(1)} %pad_maximum_fusion.12), channel_id=1, source_target_pairs={{16,24},{17,25},{18,26},{19,27},{20,28},{21,29},{22,30},{23,31}} | collective-permute-start | bytes 786440 | tf_op jit(solution)/shard_map/ppermute | solution.py:160
  295.9 1.6 copy-start.3
Sparse Core Ops, SparseCore 0:
  48.4 66.3 all-reduce.3
  171.4 69.6 all-reduce.5
